TPU v7x, 32 devices: a whole 2x2x4 slice. The times are simulated.
32 devices in a mesh: lat: 8 (over y, x, core), lon: 4 (over z).
Axes of the slice: x: 2, y: 2, z: 4, core: 2. Of those that a mesh axis runs over, the one named last changes fastest.
Arguments:
- tracer: float32 [32, 256, 2048], P(None, 'lat', 'lon'), may hold values from -6 to 6
- source: int32 [256, 16], P('lat', 'lon'), may hold values from 0 to 4095, as said below
- offset: int32 [256, 2048], P('lat', 'lon'), may hold values from 1 to 125
- fraction: float32 [256, 2048], P('lat', 'lon'), may hold values from 0 to 1
- cutoffs: int32 [2, 8], replicated, may hold values from 2 to 255
Outputs:
- advected: float32 [32, 256, 2048], P(None, 'lat', 'lon')
Inputs may be any that keep to these rules, and one draw needn't show every extreme that they name: With source[j, b] = rho * 16 + beta: |rho - j| <= 2, and some arrival blocks reach 2 in both directions. Rows j with 8 <= j < 248 have beta equal to b - 1, b or b + 1 modulo 16. Rows within 8 of a pole have rho within the same band of 8 rows at that pole and beta anywhere on the circle.
All inputs are finite; a program needn't handle non-finite values.
Results may differ from a plain program's by a relative error of at most 0.000071.
Values sent between devices are 32-bit elements; how exact they have to be, the bound alone decides.
A program may use at most 128 MiB of HBM per device.

v0:
```python
import functools
import math

import jax
import jax.numpy as jnp
import numpy as np
from jax import lax
from jax.experimental import pallas as pl
from jax.experimental.pallas import tpu as pltpu
from jax.sharding import PartitionSpec as P

NLON = 2048
BLK = 128
HL = 2
PROWS = 8
NBLK = NLON // BLK
SUB = 8
HALF = NBLK // 2 + 1
MESH = pl.DeviceIdType.MESH


def dft_tables():
    lanes = np.arange(BLK)
    angles = 2.0 * math.pi * (np.outer(lanes, lanes) % BLK) / BLK
    cosines, sines = np.cos(angles), np.sin(angles)
    matrix = np.block([[cosines, -sines], [sines, cosines]])
    turns = 2.0 * math.pi * np.outer(np.arange(NBLK), lanes) / NLON
    twiddle = np.stack([np.cos(turns), np.sin(turns)])
    return matrix.astype(np.float32), twiddle.astype(np.float32)


def add(left, right):
    if left is None:
        return right
    return left if right is None else left + right


def sub(left, right):
    if right is None:
        return left
    return -right if left is None else left - right


def scaled(value, factor):
    return None if value is None or factor == 0.0 else value * factor


def turned(value, cosine, sine):
    re, im = value
    cosine, sine = (0.0 if abs(v) < 1e-12 else v for v in (cosine, sine))
    if sine == 0.0 and cosine == 1.0:
        return value
    if cosine == 0.0 and abs(sine) == 1.0:
        if sine > 0:
            return (None if im is None else -im), re
        return im, (None if re is None else -re)
    return sub(scaled(re, cosine), scaled(im, sine)), add(scaled(re, sine), scaled(im, cosine))


def fourier(values, sign):
    count = len(values)
    if count == 1:
        return values
    even, odd = fourier(values[::2], sign), fourier(values[1::2], sign)
    low, high = [], []
    for k in range(count // 2):
        angle = sign * 2.0 * math.pi * k / count
        re, im = turned(odd[k], math.cos(angle), math.sin(angle))
        low.append((add(even[k][0], re), add(even[k][1], im)))
        high.append((sub(even[k][0], re), sub(even[k][1], im)))
    return low + high


def weights_of(t):
    return (
        -t * (t - 1.0) * (t - 2.0) / 6.0,
        (t + 1.0) * (t - 1.0) * (t - 2.0) / 2.0,
        -(t + 1.0) * t * (t - 2.0) / 2.0,
        (t + 1.0) * t * (t - 1.0) / 6.0,
    )


def wide(row):
    return jnp.broadcast_to(row, (SUB, BLK))


def lanes_at(values, index):
    return jnp.take_along_axis(values, index, axis=1, mode="promise_in_bounds")


def row_of(values, row):
    index = jnp.full((SUB, BLK), row, jnp.int32)
    return jnp.take_along_axis(values, index, axis=0, mode="promise_in_bounds")


def cubic_limited(values, anchor, weights):
    before = lanes_at(values, anchor - 1)
    here = lanes_at(values, anchor)
    after = lanes_at(values, anchor + 1)
    beyond = lanes_at(values, anchor + 2)
    mixed = weights[0] * before + weights[1] * here + weights[2] * after + weights[3] * beyond
    return jnp.minimum(jnp.maximum(mixed, jnp.minimum(here, after)), jnp.maximum(here, after))


def lanes(block):
    return pl.ds(pl.multiple_of(block * BLK, BLK), BLK)


def kernel(
    n_lat, n_lon, src_h, cut_h, trc_h, off_h, frac_h, mat_h, twd_h, out,
    src_s, cut_s, trc, off, frac, mat, twd,
    mid, side_0, side_1, side_2, side_3, ring, ids, ids_out, fracs, ids_s, lim, spec, done, back,
    halo_send, halo_recv, pol_send, pol_recv, idx_send, idx_recv, frc_send, frc_recv,
    ret_send, ret_recv, loc_sem,
):
    sides = (side_0, side_1, side_2, side_3)
    channels, rows, cells = trc.shape
    nb = cells // BLK
    groups = channels // SUB
    shares = n_lon // groups
    work_rows = PROWS // shares
    tall = work_rows * SUB
    lat, lon = lax.axis_index("lat"), lax.axis_index("lon")
    first_row = lat * rows
    first_block = lon * nb
    right, left = lax.rem(lon + 1, n_lon), lax.rem(lon + n_lon - 1, n_lon)
    down, up = lax.rem(lat + 1, n_lat), lax.rem(lat + n_lat - 1, n_lat)
    polar = (lat == 0) | (lat == n_lat - 1)
    slab = jnp.where(lat == 0, 0, rows - PROWS)
    worker = (lat == 2) | (lat == n_lat - 3)
    northern = lat < n_lat // 2
    mate = jnp.where(northern, 2 - lat, 2 * n_lat - 4 - lat)
    pole = jnp.where(northern, 0, 1)
    peers = [lax.rem(lon + d, n_lon) for d in range(n_lon)]

    edges = sorted({0, nb - 1})
    middle = list(range(1, nb - 1))

    def local(src, dst, sem):
        return pltpu.make_async_copy(src, dst, loc_sem.at[sem])

    def block_span(first_block_in, count):
        return pl.ds(first_block_in * BLK, count * BLK)

    loads = [
        local(trc_h.at[:, :, block_span(b, 1)], trc.at[:, :, block_span(b, 1)], n)
        for n, b in enumerate(edges)
    ]
    small = [local(off_h, off, 2), local(frac_h, frac, 3), local(src_h, src_s, 4)]
    tables = [local(cut_h, cut_s, 5), local(mat_h, mat, 6), local(twd_h, twd, 7)]
    for copy in loads:
        copy.start()
    centre = []
    if middle:
        span = block_span(1, len(middle))
        centre = [local(trc_h.at[:, :, span], trc.at[:, :, span], 8)]
    for copy in small + centre:
        copy.start()

    @pl.when(worker)
    def _():
        for copy in tables:
            copy.start()

    barrier = pltpu.get_barrier_semaphore()
    for device in ((lat, left), (lat, right), (up, lon), (down, lon)):
        pl.semaphore_signal(barrier, inc=1, device_id=device, device_id_type=MESH)

    @pl.when(polar | worker)
    def _():
        for peer in peers:
            pl.semaphore_signal(barrier, inc=1, device_id=(mate, peer), device_id_type=MESH)

    def turn(blocks):
        @pl.loop(0, groups * (rows // SUB))
        def _(step):
            ch = pl.multiple_of(lax.rem(step, groups) * SUB, SUB)
            row = pl.multiple_of(lax.div(step, groups) * SUB, SUB)
            for b in blocks:
                tile = trc[pl.ds(ch, SUB), pl.ds(row, SUB), b * BLK : (b + 1) * BLK]
                mid[pl.ds(HL + row, SUB), b, pl.ds(ch, SUB), :] = jnp.swapaxes(tile, 0, 1)

    for copy in loads:
        copy.wait()
    turn(edges)

    pl.semaphore_wait(barrier, jnp.where(polar | worker, 4 + n_lon, 4))

    def group_of(place):
        return pl.multiple_of(lax.rem(place, groups) * SUB, SUB)

    def span_of(place):
        return pl.ds(place * nb, nb)

    def remote(src, dst, send, recv, device):
        return pltpu.make_async_remote_copy(
            src_ref=src, dst_ref=dst, send_sem=send, recv_sem=recv,
            device_id=device, device_id_type=MESH,
        )

    slab_at = pl.ds(pl.multiple_of(slab, SUB), PROWS)
    own = span_of(lon)
    ring_copies, back_copies = [], []
    for d, peer in enumerate(peers):
        ring_copies += [
            remote(ids_out, ids.at[lon], idx_send.at[d], idx_recv.at[d], (mate, peer)),
            remote(frac.at[slab_at], fracs.at[lon], frc_send.at[d], frc_recv.at[d], (mate, peer)),
            remote(
                mid.at[pl.ds(HL + slab, PROWS), :, pl.ds(group_of(peer), SUB), :],
                ring.at[:, own],
                pol_send.at[d], pol_recv.at[d], (mate, peer),
            ),
        ]
        back_copies.append(
            remote(
                done.at[:, span_of(peer)],
                back.at[
                    pl.ds(lax.div(lon, groups) * work_rows, work_rows), :, pl.ds(group_of(lon), SUB), :
                ],
                ret_send.at[d], ret_recv.at[d], (mate, peer),
            )
        )

    first, last = 0, nb - 1
    top, bottom = pl.ds(HL, HL), pl.ds(rows, HL)
    over, under = pl.ds(0, HL), pl.ds(HL + rows, HL)
    inner = pl.ds(2 * HL, rows - 2 * HL)
    some = pl.ds(jnp.where(lat == 0, PROWS, 2 * HL), rows - PROWS)
    has_up, has_down = lat > 0, lat < n_lat - 1
    counter = iter(range(100))

    def halo(src, dst, device):
        n = next(counter)
        return remote(src, dst, halo_send.at[n], halo_recv.at[n], device)

    lat_halos = [
        (has_down, has_up, halo(mid.at[bottom], mid.at[over], (down, lon))),
        (has_up, has_down, halo(mid.at[top], mid.at[under], (up, lon))),
    ]
    lon_halos, rims, passed = [], [], []
    for g in range(groups):
        chans, side = pl.ds(g * SUB, SUB), sides[g]
        copies = []
        for to, block, half in ((right, last, 0), (left, first, 1)):
            n = next(counter)
            for span, when in ((inner, jnp.logical_not(polar)), (some, polar)):
                copies.append((when, when, remote(
                    mid.at[span, block, chans], side.at[half, span],
                    halo_send.at[n], halo_recv.at[n], (lat, to),
                )))
            for span, when in ((top, has_up), (bottom, has_down)):
                rims.append((when, when, halo(
                    mid.at[span, block, chans], side.at[half, span], (lat, to))))
            forward = [
                (has_down, has_up, halo(side.at[half, bottom], side.at[half, over], (down, lon))),
                (has_up, has_down, halo(side.at[half, top], side.at[half, under], (up, lon))),
            ]
            passed += forward
            copies += forward
        lon_halos.append(copies)

    def gated(condition, action):
        @pl.when(condition)
        def _():
            action()

    for copy in small:
        copy.wait()

    @pl.when(polar)
    def _():
        for copy in centre:
            copy.wait()
        if middle:
            turn(middle)
        ids_out[0:PROWS] = off[slab_at]
        placed = jnp.zeros((PROWS, BLK), jnp.int32)
        row_ids = lax.broadcasted_iota(jnp.int32, (PROWS, BLK), 0)
        lane_ids = lax.broadcasted_iota(jnp.int32, (PROWS, BLK), 1)
        for j in range(PROWS):
            for b in range(nb):
                placed = jnp.where((row_ids == j) & (lane_ids == b), src_s[b, slab + j], placed)
        ids_out[PROWS : 2 * PROWS, 0:BLK] = placed
        if nb > 1:
            ids_out[PROWS : 2 * PROWS, BLK:] = jnp.zeros((PROWS, cells - BLK), jnp.int32)
        for copy in ring_copies:
            copy.start()

    for sends, _, copy in rims:
        gated(sends, copy.start)
    for copies in lon_halos:
        for sends, _, copy in copies:
            if all(copy is not other for _, _, other in passed):
                gated(sends, copy.start)

    @pl.when(jnp.logical_not(polar))
    def _():
        for copy in centre:
            copy.wait()
        if middle:
            turn(middle)

    for sends, _, copy in lat_halos:
        gated(sends, copy.start)

    def tile(group, b, edge, chosen):
        row = pl.multiple_of(group * SUB, SUB)
        at = lanes(b)
        weights = weights_of(frac[pl.ds(row, SUB), at])
        anchors = off[pl.ds(row, SUB), at]
        results = {g: [] for g in chosen}
        for j in range(SUB):
            block_id = src_s[b, row + j]
            source_row = lax.div(block_id, NBLK) - first_row + HL
            source_row = jnp.clip(source_row, 0, rows + 2 * HL - 1)
            place = lax.rem(lax.rem(block_id, NBLK) - first_block + 1 + NBLK, NBLK)
            near = jnp.clip(place - 1, 0, nb - 1)
            far = jnp.minimum(place, 1)
            spot = jnp.full((SUB, BLK), place, jnp.int32)
            inside = (spot >= 1) & (spot <= nb)
            anchor = wide(anchors[j : j + 1])
            factors = [wide(w[j : j + 1]) for w in weights]
            for g in chosen:
                values = mid[source_row, near, pl.ds(g * SUB, SUB), :]
                if edge:
                    values = jnp.where(inside, values, sides[g][far, source_row])
                results[g].append(cubic_limited(values, anchor, factors))
        for g in chosen:
            out[g * SUB : (g + 1) * SUB, pl.ds(row, SUB), at] = jnp.swapaxes(
                jnp.stack(results[g]), 0, 1
            )

    tiles = rows // SUB

    def sweep(blocks, edge, chosen):
        count = len(blocks)
        if not count:
            return
        start, stride = blocks[0], (blocks[1] - blocks[0] if count > 1 else 1)

        @pl.loop(0, tiles * count)
        def _(step):
            group = lax.div(step, count)
            at_pole = ((lat == 0) & (group == 0)) | ((lat == n_lat - 1) & (group == tiles - 1))

            @pl.when(jnp.logical_not(at_pole))
            def _():
                tile(group, start + stride * lax.rem(step, count), edge, chosen)

    for _, receives, copy in rims:
        gated(receives, copy.wait_recv)
    for sends, _, copy in passed:
        gated(sends, copy.start)
    for _, receives, copy in lat_halos:
        gated(receives, copy.wait_recv)
    sweep(middle, False, range(groups))

    @pl.when(worker)
    def _():
        for copy in tables:
            copy.wait()
        for copy in ring_copies:
            copy.wait_recv()
        fetch = pltpu.make_async_copy(
            ids.at[:, pl.ds(PROWS, PROWS), pl.ds(0, BLK)], ids_s, loc_sem.at[9]
        )
        fetch.start()
        fetch.wait()
        row_base = lax.div(lon, groups) * work_rows
        slab_global = jnp.where(northern, 0, n_lat * rows - PROWS)

        @pl.loop(0, work_rows)
        def _(j):
            jw = row_base + j
            band = []
            for b in range(NBLK):
                q, bb = b // nb, b % nb
                block_id = ids_s[q, jw, bb]
                source_row = jnp.clip(lax.div(block_id, NBLK) - slab_global, 0, PROWS - 1)
                values = ring[source_row, lax.rem(block_id, NBLK)]
                at = pl.ds(bb * BLK, BLK)
                weights = weights_of(row_of(fracs[q, :, at], jw))
                anchor = row_of(ids[q, 0:PROWS, at], jw)
                limited = cubic_limited(values, anchor, weights)
                lim[j, b] = limited
                band.append((limited, None))
            waves = fourier(band, -1)
            for k in range(HALF):
                re, im = waves[k]
                cosine, sine = wide(twd[0, k : k + 1, :]), wide(twd[1, k : k + 1, :])
                at = pl.ds(pl.multiple_of(k * tall + j * SUB, SUB), SUB)
                if im is None:
                    spec[at, 0:BLK] = re * cosine
                    spec[at, BLK : 2 * BLK] = -re * sine
                else:
                    spec[at, 0:BLK] = re * cosine + im * sine
                    spec[at, BLK : 2 * BLK] = im * cosine - re * sine

        def transform():
            spec[...] = jnp.dot(
                spec[...], mat[...], precision=lax.Precision.HIGHEST,
                preferred_element_type=jnp.float32,
            )

        transform()

        @pl.loop(0, work_rows)
        def _(j):
            kappa = cut_s[pole, row_base + j].astype(jnp.float32)
            for k in range(HALF):
                wave = k + NBLK * lax.broadcasted_iota(jnp.int32, (SUB, BLK), 1)
                wave = jnp.minimum(wave, NLON - wave)
                kept = (wave >= 1) & (wave < NLON // 2)
                damping = 1.0 - kappa / jnp.maximum(wave, 1).astype(jnp.float32)
                damping = jnp.where(kept, jnp.maximum(damping, 0.0), 0.0) * (1.0 / NLON)
                at = pl.ds(pl.multiple_of(k * tall + j * SUB, SUB), SUB)
                spec[at, 0:BLK] = spec[at, 0:BLK] * damping
                spec[at, BLK : 2 * BLK] = -spec[at, BLK : 2 * BLK] * damping

        transform()

        @pl.loop(0, work_rows)
        def _(j):
            waves = []
            for k in range(HALF):
                at = pl.ds(pl.multiple_of(k * tall + j * SUB, SUB), SUB)
                re, im = spec[at, 0:BLK], spec[at, BLK : 2 * BLK]
                cosine, sine = wide(twd[0, k : k + 1, :]), wide(twd[1, k : k + 1, :])
                real = re * cosine + im * sine
                waves.append((real, None if k in (0, HALF - 1) else re * sine - im * cosine))
            for k in range(HALF, NBLK):
                re, im = waves[NBLK - k]
                waves.append((re, -im))
            removed = fourier(waves, 1)
            for b in range(NBLK):
                done[j, b] = lim[j, b] - removed[b][0]

        for copy in back_copies:
            copy.start()

    for g, copies in enumerate(lon_halos):
        for _, receives, copy in copies:
            gated(receives, copy.wait_recv)
        sweep(edges, True, [g])

    @pl.when(polar)
    def _():
        for copy in back_copies:
            copy.wait_recv()

        @pl.loop(0, groups)
        def _(g):
            ch = pl.multiple_of(g * SUB, SUB)
            for b in range(nb):
                at = slice(b * BLK, (b + 1) * BLK)
                out[pl.ds(ch, SUB), slab_at, at] = jnp.swapaxes(back[:, b, pl.ds(ch, SUB), :], 0, 1)

        for copy in ring_copies:
            copy.wait_send()

    @pl.when(worker)
    def _():
        for copy in back_copies:
            copy.wait_send()

    for sends, _, copy in lat_halos + rims + sum(lon_halos, []):
        gated(sends, copy.wait_send)


def body(n_lat, n_lon, tracer, source, offset, fraction, cutoffs):
    channels, rows, cells = tracer.shape
    shares = n_lon // (channels // SUB)
    work_rows = PROWS // shares
    matrix, twiddle = dft_tables()
    dma = pltpu.SemaphoreType.DMA
    vmem = pl.BlockSpec(memory_space=pltpu.VMEM)
    return pl.pallas_call(
        functools.partial(kernel, n_lat, n_lon),
        out_shape=jax.ShapeDtypeStruct(tracer.shape, jnp.float32),
        in_specs=[pl.BlockSpec(memory_space=pltpu.HBM)] * 7,
        out_specs=vmem,
        scratch_shapes=[
            pltpu.SMEM(source.shape[::-1], jnp.int32),
            pltpu.SMEM(cutoffs.shape, jnp.int32),
            pltpu.VMEM(tracer.shape, jnp.float32),
            pltpu.VMEM(offset.shape, jnp.int32),
            pltpu.VMEM(fraction.shape, jnp.float32),
            pltpu.VMEM(matrix.shape, jnp.float32),
            pltpu.VMEM(twiddle.shape, jnp.float32),
            pltpu.VMEM((rows + 2 * HL, cells // BLK, channels, BLK), jnp.float32),
        ] + [pltpu.VMEM((2, rows + 2 * HL, SUB, BLK), jnp.float32)] * 4 + [
            pltpu.VMEM((PROWS, NBLK, SUB, BLK), jnp.float32),
            pltpu.VMEM((n_lon, 2 * PROWS, cells), jnp.int32),
            pltpu.VMEM((2 * PROWS, cells), jnp.int32),
            pltpu.VMEM((n_lon, PROWS, cells), jnp.float32),
            pltpu.SMEM((n_lon, PROWS, BLK), jnp.int32),
            pltpu.VMEM((work_rows, NBLK, SUB, BLK), jnp.float32),
            pltpu.VMEM((HALF * work_rows * SUB, 2 * BLK), jnp.float32),
            pltpu.VMEM((work_rows, NBLK, SUB, BLK), jnp.float32),
            pltpu.VMEM((PROWS, cells // BLK, channels, BLK), jnp.float32),
            dma((42,)), dma((42,)),
        ] + [dma((n_lon,))] * 8 + [dma((10,))],
        compiler_params=pltpu.CompilerParams(
            collective_id=0, has_side_effects=True, vmem_limit_bytes=64 * 2**20 - 2**16
        ),
        cost_estimate=pl.CostEstimate(flops=10**9, bytes_accessed=5 * 10**6, transcendentals=0),
    )(source.T, cutoffs, tracer, offset, fraction, jnp.asarray(matrix), jnp.asarray(twiddle))


def solution(mesh):
    placed = (P(None, "lat", "lon"), P("lat", "lon"), P("lat", "lon"), P("lat", "lon"), P())
    step = functools.partial(body, mesh.shape["lat"], mesh.shape["lon"])
    return jax.shard_map(
        step, mesh=mesh, in_specs=placed, out_specs=P(None, "lat", "lon"), check_vma=False
    )
```

profile of v0, /device:TPU:0, one launch (start us, length us, event | category | flops | bytes accessed | tf_op | source)
XLA Modules:
  0.0 43.3 jit_solution(1011822058055304893)
XLA Ops:
  0.0 40.1 %shard_map.73 = f32[32,32,512]{2,1,0:T(8,128)} custom-call(s32[4,32]{1,0:T(4,128)} %bitcast.1, s32[2,8]{1,0:T(2,128)} %cut_h.1, f32[32,32,512]{2,1,0:T(8,128)} %trc_h.1, s32[32,512]{1,0:T(8,128)} %off_h.1, f32[32,512]{1,0:T(8,128)} %frac_h.1, f32[256,256]{1,0:T(8,128)} %constant.4.clone.mat_h, f32[2,16,128]{2,1,0:T(8,128)} %constant.5.clone.twd_h), custom_call_target="tpu_custom_call" | custom-call | flops 1000000000 | bytes 5000000 | tf_op jit(solution)/shard_map/pallas_call | solution.py:477
  40.2 3.2 %copy.9 = f32[32,32,512]{2,1,0:T(8,128)} copy(f32[32,32,512]{2,1,0:T(8,128)} %shard_map.73) | data formatting | bytes 4194304
where the time goes:
time: 44 us; the launch traced here: 43.3 us
  Pallas kernels  40.1 us (91%)
  local copies, waits for them, and re-layouts  3.19 us (7%)
    pallas_call x1, Pallas kernels, body(): pl.pallas_call(functools.partial(kernel, n_lat, n_lon), out_shape=jax.Sha...  40.1 us
    unnamed x1, local copies, waits for them, and re-layouts  3.19 us

commit v1 on v0

--- a/solution.py
+++ b/solution.py
@@ -17,6 +17,7 @@
 SUB = 8
 HALF = NBLK // 2 + 1
 MESH = pl.DeviceIdType.MESH
+VMEM_LIMIT = 64 * 2**20 - 2**16
 
 
 def dft_tables():
@@ -78,6 +79,11 @@
         -(t + 1.0) * t * (t - 2.0) / 2.0,
         (t + 1.0) * t * (t - 1.0) / 6.0,
     )
+
+
+def halves(values):
+    upper = values.astype(jnp.bfloat16)
+    return upper, (values - upper.astype(jnp.float32)).astype(jnp.bfloat16)
 
 
 def wide(row):
@@ -171,18 +177,36 @@
         for peer in peers:
             pl.semaphore_signal(barrier, inc=1, device_id=(mate, peer), device_id_type=MESH)
 
-    def turn(blocks):
-        @pl.loop(0, groups * (rows // SUB))
+    def turn(blocks, row_groups, skip_pole):
+        @pl.loop(0, groups * len(row_groups))
         def _(step):
             ch = pl.multiple_of(lax.rem(step, groups) * SUB, SUB)
-            row = pl.multiple_of(lax.div(step, groups) * SUB, SUB)
-            for b in blocks:
-                tile = trc[pl.ds(ch, SUB), pl.ds(row, SUB), b * BLK : (b + 1) * BLK]
-                mid[pl.ds(HL + row, SUB), b, pl.ds(ch, SUB), :] = jnp.swapaxes(tile, 0, 1)
-
+            index = lax.div(step, groups)
+            row = pl.multiple_of(index * SUB if len(row_groups) > 1 else row_groups[0], SUB)
+
+            def move():
+                for b in blocks:
+                    tile = trc[pl.ds(ch, SUB), pl.ds(row, SUB), b * BLK : (b + 1) * BLK]
+                    mid[pl.ds(HL + row, SUB), b, pl.ds(ch, SUB), :] = jnp.swapaxes(tile, 0, 1)
+
+            if skip_pole:
+                pl.when(jnp.logical_not(polar & (row == slab)))(move)
+            else:
+                move()
+
+    every = range(rows // SUB)
     for copy in loads:
         copy.wait()
-    turn(edges)
+
+    @pl.when(polar)
+    def _():
+        for copy in centre:
+            copy.wait()
+        turn(edges + middle, [slab], False)
+
+    @pl.when(jnp.logical_not(polar))
+    def _():
+        turn(edges, every, False)
 
     pl.semaphore_wait(barrier, jnp.where(polar | worker, 4 + n_lon, 4))
 
@@ -269,10 +293,6 @@
 
     @pl.when(polar)
     def _():
-        for copy in centre:
-            copy.wait()
-        if middle:
-            turn(middle)
         ids_out[0:PROWS] = off[slab_at]
         placed = jnp.zeros((PROWS, BLK), jnp.int32)
         row_ids = lax.broadcasted_iota(jnp.int32, (PROWS, BLK), 0)
@@ -285,20 +305,25 @@
             ids_out[PROWS : 2 * PROWS, BLK:] = jnp.zeros((PROWS, cells - BLK), jnp.int32)
         for copy in ring_copies:
             copy.start()
+        turn(edges + middle, every, True)
+
+    def send_group(g):
+        for sends, _, copy in lon_halos[g]:
+            if all(copy is not other for _, _, other in passed):
+                gated(sends, copy.start)
 
     for sends, _, copy in rims:
         gated(sends, copy.start)
-    for copies in lon_halos:
-        for sends, _, copy in copies:
-            if all(copy is not other for _, _, other in passed):
-                gated(sends, copy.start)
+    ahead = 2
+    for g in range(ahead):
+        send_group(g)
 
     @pl.when(jnp.logical_not(polar))
     def _():
         for copy in centre:
             copy.wait()
         if middle:
-            turn(middle)
+            turn(middle, every, False)
 
     for sends, _, copy in lat_halos:
         gated(sends, copy.start)
@@ -397,9 +422,11 @@
                     spec[at, BLK : 2 * BLK] = im * cosine - re * sine
 
         def transform():
-            spec[...] = jnp.dot(
-                spec[...], mat[...], precision=lax.Precision.HIGHEST,
-                preferred_element_type=jnp.float32,
+            upper, lower = halves(spec[...])
+            mat_upper, mat_lower = halves(mat[...])
+            product = functools.partial(jnp.dot, preferred_element_type=jnp.float32)
+            spec[...] = product(upper, mat_upper) + (
+                product(lower, mat_upper) + product(upper, mat_lower)
             )
 
         transform()
@@ -441,6 +468,8 @@
     for g, copies in enumerate(lon_halos):
         for _, receives, copy in copies:
             gated(receives, copy.wait_recv)
+        if g + ahead < groups:
+            send_group(g + ahead)
         sweep(edges, True, [g])
 
     @pl.when(polar)
@@ -465,6 +494,10 @@
 
     for sends, _, copy in lat_halos + rims + sum(lon_halos, []):
         gated(sends, copy.wait_send)
+
+
+def write_out(values, out):
+    out[...] = values[...]
 
 
 def body(n_lat, n_lon, tracer, source, offset, fraction, cutoffs):
@@ -474,7 +507,7 @@
     matrix, twiddle = dft_tables()
     dma = pltpu.SemaphoreType.DMA
     vmem = pl.BlockSpec(memory_space=pltpu.VMEM)
-    return pl.pallas_call(
+    result = pl.pallas_call(
         functools.partial(kernel, n_lat, n_lon),
         out_shape=jax.ShapeDtypeStruct(tracer.shape, jnp.float32),
         in_specs=[pl.BlockSpec(memory_space=pltpu.HBM)] * 7,
@@ -501,10 +534,20 @@
             dma((42,)), dma((42,)),
         ] + [dma((n_lon,))] * 8 + [dma((10,))],
         compiler_params=pltpu.CompilerParams(
-            collective_id=0, has_side_effects=True, vmem_limit_bytes=64 * 2**20 - 2**16
+            collective_id=0, has_side_effects=True, vmem_limit_bytes=VMEM_LIMIT
         ),
         cost_estimate=pl.CostEstimate(flops=10**9, bytes_accessed=5 * 10**6, transcendentals=0),
     )(source.T, cutoffs, tracer, offset, fraction, jnp.asarray(matrix), jnp.asarray(twiddle))
+    block = pl.BlockSpec((SUB, rows, cells), lambda g: (g, 0, 0))
+    return pl.pallas_call(
+        write_out,
+        out_shape=jax.ShapeDtypeStruct(tracer.shape, jnp.float32),
+        grid=(channels // SUB,),
+        in_specs=[block],
+        out_specs=block,
+        compiler_params=pltpu.CompilerParams(vmem_limit_bytes=VMEM_LIMIT),
+        cost_estimate=pl.CostEstimate(flops=0, bytes_accessed=4 * 10**6, transcendentals=0),
+    )(result)
 
 
 def solution(mesh):

time: 44 us -> 45 us (1.023)
  the two profiles are of different devices: /device:TPU:0 before, /device:TPU:18 now
where the time goes in v1:
time: 45 us; the launch traced here: 44.8 us
  Pallas kernels  44.8 us (100%)
    pallas_call x1, Pallas kernels, body(): pl.pallas_call(functools.partial(kernel, n_lat, n_lon), out_shape=jax.Sha...  41 us
    pallas_call x1, Pallas kernels, body(): pl.pallas_call(write_out, out_shape=jax.ShapeDtypeStruct(tracer.shape, jn...  3.78 us

profile of v1, /device:TPU:18, one launch (start us, length us, event | category | flops | bytes accessed | tf_op | source)
XLA Modules:
  0.0 44.8 jit_solution(86919649365540437)
XLA Ops:
  0.0 41.0 %shard_map.73.values = f32[32,32,512]{2,1,0:T(8,128)} custom-call(s32[4,32]{1,0:T(4,128)} %bitcast.1, s32[2,8]{1,0:T(2,128)} %cut_h.1, f32[32,32,512]{2,1,0:T(8,128)} %trc_h.1, s32[32,512]{1,0:T(8,128)} %off_h.1, f32[32,512]{1,0:T(8,128)} %frac_h.1, f32[256,256]{1,0:T(8,128)} %constant.4.clone.mat_h, f32[2,16,128]{2,1,0:T(8,128)} %constant.5.clone.twd_h), custom_call_target="tpu_custom_call" | custom-call | flops 1000000000 | bytes 5000000 | tf_op jit(solution)/shard_map/pallas_call | solution.py:510
  41.1 3.8 %shard_map.74 = f32[32,32,512]{2,1,0:T(8,128)} custom-call(f32[32,32,512]{2,1,0:T(8,128)} %shard_map.73.values), custom_call_target="tpu_custom_call" | custom-call | bytes 4000000 | tf_op jit(solution)/shard_map/pallas_call | solution.py:542

commit v2 on v1

--- a/solution.py
+++ b/solution.py
@@ -17,7 +17,7 @@
 SUB = 8
 HALF = NBLK // 2 + 1
 MESH = pl.DeviceIdType.MESH
-VMEM_LIMIT = 64 * 2**20 - 2**16
+VMEM_LIMIT = 48 * 2**20
 
 
 def dft_tables():
@@ -115,7 +115,7 @@
 def kernel(
     n_lat, n_lon, src_h, cut_h, trc_h, off_h, frac_h, mat_h, twd_h, out,
     src_s, cut_s, trc, off, frac, mat, twd,
-    mid, side_0, side_1, side_2, side_3, ring, ids, ids_out, fracs, ids_s, lim, spec, done, back,
+    mid, side_0, side_1, side_2, side_3, ring, ids, ids_out, fracs, ids_s, coef, anch, damp, lim, spec, done, back,
     halo_send, halo_recv, pol_send, pol_recv, idx_send, idx_recv, frc_send, frc_recv,
     ret_send, ret_recv, loc_sem,
 ):
@@ -314,7 +314,7 @@
 
     for sends, _, copy in rims:
         gated(sends, copy.start)
-    ahead = 2
+    ahead = groups
     for g in range(ahead):
         send_group(g)
 
@@ -384,15 +384,35 @@
     def _():
         for copy in tables:
             copy.wait()
-        for copy in ring_copies:
-            copy.wait_recv()
+        for n in range(0, len(ring_copies), 3):
+            ring_copies[n].wait_recv()
+            ring_copies[n + 1].wait_recv()
         fetch = pltpu.make_async_copy(
             ids.at[:, pl.ds(PROWS, PROWS), pl.ds(0, BLK)], ids_s, loc_sem.at[9]
         )
         fetch.start()
-        fetch.wait()
         row_base = lax.div(lon, groups) * work_rows
         slab_global = jnp.where(northern, 0, n_lat * rows - PROWS)
+
+        @pl.loop(0, work_rows)
+        def _(j):
+            jw = row_base + j
+            for b in range(NBLK):
+                q, at = b // nb, pl.ds(b % nb * BLK, BLK)
+                for n, weight in enumerate(weights_of(row_of(fracs[q, :, at], jw))):
+                    coef[j, b, n] = weight
+                anch[j, b] = row_of(ids[q, 0:PROWS, at], jw)
+            kappa = cut_s[pole, jw].astype(jnp.float32)
+            for k in range(HALF):
+                wave = k + NBLK * lax.broadcasted_iota(jnp.int32, (SUB, BLK), 1)
+                wave = jnp.minimum(wave, NLON - wave)
+                kept = (wave >= 1) & (wave < NLON // 2)
+                damping = 1.0 - kappa / jnp.maximum(wave, 1).astype(jnp.float32)
+                damp[j, k] = jnp.where(kept, jnp.maximum(damping, 0.0), 0.0) * (1.0 / NLON)
+
+        fetch.wait()
+        for n in range(2, len(ring_copies), 3):
+            ring_copies[n].wait_recv()
 
         @pl.loop(0, work_rows)
         def _(j):
@@ -403,10 +423,7 @@
                 block_id = ids_s[q, jw, bb]
                 source_row = jnp.clip(lax.div(block_id, NBLK) - slab_global, 0, PROWS - 1)
                 values = ring[source_row, lax.rem(block_id, NBLK)]
-                at = pl.ds(bb * BLK, BLK)
-                weights = weights_of(row_of(fracs[q, :, at], jw))
-                anchor = row_of(ids[q, 0:PROWS, at], jw)
-                limited = cubic_limited(values, anchor, weights)
+                limited = cubic_limited(values, anch[j, b], [coef[j, b, n] for n in range(4)])
                 lim[j, b] = limited
                 band.append((limited, None))
             waves = fourier(band, -1)
@@ -433,13 +450,8 @@
 
         @pl.loop(0, work_rows)
         def _(j):
-            kappa = cut_s[pole, row_base + j].astype(jnp.float32)
             for k in range(HALF):
-                wave = k + NBLK * lax.broadcasted_iota(jnp.int32, (SUB, BLK), 1)
-                wave = jnp.minimum(wave, NLON - wave)
-                kept = (wave >= 1) & (wave < NLON // 2)
-                damping = 1.0 - kappa / jnp.maximum(wave, 1).astype(jnp.float32)
-                damping = jnp.where(kept, jnp.maximum(damping, 0.0), 0.0) * (1.0 / NLON)
+                damping = damp[j, k]
                 at = pl.ds(pl.multiple_of(k * tall + j * SUB, SUB), SUB)
                 spec[at, 0:BLK] = spec[at, 0:BLK] * damping
                 spec[at, BLK : 2 * BLK] = -spec[at, BLK : 2 * BLK] * damping
@@ -496,18 +508,17 @@
         gated(sends, copy.wait_send)
 
 
-def write_out(values, out):
-    out[...] = values[...]
-
-
 def body(n_lat, n_lon, tracer, source, offset, fraction, cutoffs):
     channels, rows, cells = tracer.shape
     shares = n_lon // (channels // SUB)
     work_rows = PROWS // shares
     matrix, twiddle = dft_tables()
+    operands = (
+        source.T, cutoffs, tracer, offset, fraction, jnp.asarray(matrix), jnp.asarray(twiddle)
+    )
     dma = pltpu.SemaphoreType.DMA
     vmem = pl.BlockSpec(memory_space=pltpu.VMEM)
-    result = pl.pallas_call(
+    return pl.pallas_call(
         functools.partial(kernel, n_lat, n_lon),
         out_shape=jax.ShapeDtypeStruct(tracer.shape, jnp.float32),
         in_specs=[pl.BlockSpec(memory_space=pltpu.HBM)] * 7,
@@ -527,6 +538,9 @@
             pltpu.VMEM((2 * PROWS, cells), jnp.int32),
             pltpu.VMEM((n_lon, PROWS, cells), jnp.float32),
             pltpu.SMEM((n_lon, PROWS, BLK), jnp.int32),
+            pltpu.VMEM((work_rows, NBLK, 4, SUB, BLK), jnp.float32),
+            pltpu.VMEM((work_rows, NBLK, SUB, BLK), jnp.int32),
+            pltpu.VMEM((work_rows, HALF, SUB, BLK), jnp.float32),
             pltpu.VMEM((work_rows, NBLK, SUB, BLK), jnp.float32),
             pltpu.VMEM((HALF * work_rows * SUB, 2 * BLK), jnp.float32),
             pltpu.VMEM((work_rows, NBLK, SUB, BLK), jnp.float32),
@@ -537,17 +551,7 @@
             collective_id=0, has_side_effects=True, vmem_limit_bytes=VMEM_LIMIT
         ),
         cost_estimate=pl.CostEstimate(flops=10**9, bytes_accessed=5 * 10**6, transcendentals=0),
-    )(source.T, cutoffs, tracer, offset, fraction, jnp.asarray(matrix), jnp.asarray(twiddle))
-    block = pl.BlockSpec((SUB, rows, cells), lambda g: (g, 0, 0))
-    return pl.pallas_call(
-        write_out,
-        out_shape=jax.ShapeDtypeStruct(tracer.shape, jnp.float32),
-        grid=(channels // SUB,),
-        in_specs=[block],
-        out_specs=block,
-        compiler_params=pltpu.CompilerParams(vmem_limit_bytes=VMEM_LIMIT),
-        cost_estimate=pl.CostEstimate(flops=0, bytes_accessed=4 * 10**6, transcendentals=0),
-    )(result)
+    )(*(pltpu.with_memory_space_constraint(value, pltpu.HBM) for value in operands))
 
 
 def solution(mesh):

time: 45 us -> 39 us (0.87)
  the two profiles are of different devices: /device:TPU:18 before, /device:TPU:0 now
where the time goes in v2:
time: 39 us; the launch traced here: 38.4 us
  Pallas kernels  37 us (95%)
  local copies, waits for them, and re-layouts  1.32 us (3%)
    pallas_call x1, Pallas kernels, body(): pl.pallas_call(functools.partial(kernel, n_lat, n_lon), out_shape=jax.Sha...  37 us
    unnamed x1, local copies, waits for them, and re-layouts  1.32 us

profile of v2, /device:TPU:0, one launch (start us, length us, event | category | flops | bytes accessed | tf_op | source)
XLA Modules:
  0.0 38.4 jit_solution(14870090437939152068)
XLA Ops:
  0.0 37.0 %shard_map.73 = f32[32,32,512]{2,1,0:T(8,128)S(1)} custom-call(s32[4,32]{1,0:T(4,128)} %bitcast.1, s32[2,8]{1,0:T(2,128)} %cut_h.1, f32[32,32,512]{2,1,0:T(8,128)} %trc_h.1, s32[32,512]{1,0:T(8,128)} %off_h.1, f32[32,512]{1,0:T(8,128)} %frac_h.1, f32[256,256]{1,0:T(8,128)} %constant.4.clone.mat_h, f32[2,16,128]{2,1,0:T(8,128)} %constant.5.clone.twd_h), custom_call_target="tpu_custom_call" | custom-call | flops 1000000000 | bytes 5000000 | tf_op jit(solution)/shard_map/pallas_call | solution.py:521
  37.0 1.3 %copy.9 = f32[32,32,512]{2,1,0:T(8,128)} copy(f32[32,32,512]{2,1,0:T(8,128)S(1)} %shard_map.73) | data formatting | bytes 4194304

commit v3 on v2

--- a/solution.py
+++ b/solution.py
@@ -16,6 +16,7 @@
 NBLK = NLON // BLK
 SUB = 8
 HALF = NBLK // 2 + 1
+PARTS = 2
 MESH = pl.DeviceIdType.MESH
 VMEM_LIMIT = 48 * 2**20
 
@@ -125,7 +126,8 @@
     groups = channels // SUB
     shares = n_lon // groups
     work_rows = PROWS // shares
-    tall = work_rows * SUB
+    part_rows = work_rows // PARTS
+    tall = part_rows * SUB
     lat, lon = lax.axis_index("lat"), lax.axis_index("lon")
     first_row = lat * rows
     first_block = lon * nb
@@ -235,15 +237,17 @@
                 pol_send.at[d], pol_recv.at[d], (mate, peer),
             ),
         ]
-        back_copies.append(
-            remote(
-                done.at[:, span_of(peer)],
-                back.at[
-                    pl.ds(lax.div(lon, groups) * work_rows, work_rows), :, pl.ds(group_of(lon), SUB), :
-                ],
-                ret_send.at[d], ret_recv.at[d], (mate, peer),
+
+    for part in range(PARTS):
+        for d, peer in enumerate(peers):
+            to_row = lax.div(lon, groups) * work_rows + part * part_rows
+            back_copies.append(
+                remote(
+                    done.at[pl.ds(part * part_rows, part_rows), span_of(peer)],
+                    back.at[pl.ds(to_row, part_rows), :, pl.ds(group_of(lon), SUB), :],
+                    ret_send.at[part * n_lon + d], ret_recv.at[part * n_lon + d], (mate, peer),
+                )
             )
-        )
 
     first, last = 0, nb - 1
     top, bottom = pl.ds(HL, HL), pl.ds(rows, HL)
@@ -307,16 +311,15 @@
             copy.start()
         turn(edges + middle, every, True)
 
-    def send_group(g):
-        for sends, _, copy in lon_halos[g]:
-            if all(copy is not other for _, _, other in passed):
-                gated(sends, copy.start)
+    def send_lon(only_polar):
+        for copies in lon_halos:
+            for sends, _, copy in copies:
+                if all(copy is not other for _, _, other in passed) and (sends is polar) == only_polar:
+                    gated(sends, copy.start)
 
     for sends, _, copy in rims:
         gated(sends, copy.start)
-    ahead = groups
-    for g in range(ahead):
-        send_group(g)
+    send_lon(False)
 
     @pl.when(jnp.logical_not(polar))
     def _():
@@ -376,9 +379,22 @@
         gated(receives, copy.wait_recv)
     for sends, _, copy in passed:
         gated(sends, copy.start)
-    for _, receives, copy in lat_halos:
-        gated(receives, copy.wait_recv)
-    sweep(middle, False, range(groups))
+
+    def inner_tiles():
+        for _, receives, copy in lat_halos:
+            gated(receives, copy.wait_recv)
+        sweep(middle, False, range(groups))
+
+    @pl.when(jnp.logical_not(worker))
+    def _():
+        inner_tiles()
+
+    @pl.when(polar)
+    def _():
+        for copy in ring_copies:
+            copy.wait_send()
+
+    send_lon(True)
 
     @pl.when(worker)
     def _():
@@ -414,30 +430,6 @@
         for n in range(2, len(ring_copies), 3):
             ring_copies[n].wait_recv()
 
-        @pl.loop(0, work_rows)
-        def _(j):
-            jw = row_base + j
-            band = []
-            for b in range(NBLK):
-                q, bb = b // nb, b % nb
-                block_id = ids_s[q, jw, bb]
-                source_row = jnp.clip(lax.div(block_id, NBLK) - slab_global, 0, PROWS - 1)
-                values = ring[source_row, lax.rem(block_id, NBLK)]
-                limited = cubic_limited(values, anch[j, b], [coef[j, b, n] for n in range(4)])
-                lim[j, b] = limited
-                band.append((limited, None))
-            waves = fourier(band, -1)
-            for k in range(HALF):
-                re, im = waves[k]
-                cosine, sine = wide(twd[0, k : k + 1, :]), wide(twd[1, k : k + 1, :])
-                at = pl.ds(pl.multiple_of(k * tall + j * SUB, SUB), SUB)
-                if im is None:
-                    spec[at, 0:BLK] = re * cosine
-                    spec[at, BLK : 2 * BLK] = -re * sine
-                else:
-                    spec[at, 0:BLK] = re * cosine + im * sine
-                    spec[at, BLK : 2 * BLK] = im * cosine - re * sine
-
         def transform():
             upper, lower = halves(spec[...])
             mat_upper, mat_lower = halves(mat[...])
@@ -446,42 +438,71 @@
                 product(lower, mat_upper) + product(upper, mat_lower)
             )
 
-        transform()
-
-        @pl.loop(0, work_rows)
-        def _(j):
-            for k in range(HALF):
-                damping = damp[j, k]
-                at = pl.ds(pl.multiple_of(k * tall + j * SUB, SUB), SUB)
-                spec[at, 0:BLK] = spec[at, 0:BLK] * damping
-                spec[at, BLK : 2 * BLK] = -spec[at, BLK : 2 * BLK] * damping
-
-        transform()
-
-        @pl.loop(0, work_rows)
-        def _(j):
-            waves = []
-            for k in range(HALF):
-                at = pl.ds(pl.multiple_of(k * tall + j * SUB, SUB), SUB)
-                re, im = spec[at, 0:BLK], spec[at, BLK : 2 * BLK]
-                cosine, sine = wide(twd[0, k : k + 1, :]), wide(twd[1, k : k + 1, :])
-                real = re * cosine + im * sine
-                waves.append((real, None if k in (0, HALF - 1) else re * sine - im * cosine))
-            for k in range(HALF, NBLK):
-                re, im = waves[NBLK - k]
-                waves.append((re, -im))
-            removed = fourier(waves, 1)
-            for b in range(NBLK):
-                done[j, b] = lim[j, b] - removed[b][0]
-
-        for copy in back_copies:
-            copy.start()
+        for part in range(PARTS):
+
+            @pl.loop(0, part_rows)
+            def _(step):
+                j = part * part_rows + step
+                jw = row_base + j
+                band = []
+                for b in range(NBLK):
+                    q, bb = b // nb, b % nb
+                    block_id = ids_s[q, jw, bb]
+                    source_row = jnp.clip(lax.div(block_id, NBLK) - slab_global, 0, PROWS - 1)
+                    values = ring[source_row, lax.rem(block_id, NBLK)]
+                    limited = cubic_limited(values, anch[j, b], [coef[j, b, n] for n in range(4)])
+                    lim[j, b] = limited
+                    band.append((limited, None))
+                waves = fourier(band, -1)
+                for k in range(HALF):
+                    re, im = waves[k]
+                    cosine, sine = wide(twd[0, k : k + 1, :]), wide(twd[1, k : k + 1, :])
+                    at = pl.ds(pl.multiple_of(k * tall + step * SUB, SUB), SUB)
+                    if im is None:
+                        spec[at, 0:BLK] = re * cosine
+                        spec[at, BLK : 2 * BLK] = -re * sine
+                    else:
+                        spec[at, 0:BLK] = re * cosine + im * sine
+                        spec[at, BLK : 2 * BLK] = im * cosine - re * sine
+
+            transform()
+
+            @pl.loop(0, part_rows)
+            def _(step):
+                j = part * part_rows + step
+                for k in range(HALF):
+                    damping = damp[j, k]
+                    at = pl.ds(pl.multiple_of(k * tall + step * SUB, SUB), SUB)
+                    spec[at, 0:BLK] = spec[at, 0:BLK] * damping
+                    spec[at, BLK : 2 * BLK] = -spec[at, BLK : 2 * BLK] * damping
+
+            transform()
+
+            @pl.loop(0, part_rows)
+            def _(step):
+                j = part * part_rows + step
+                waves = []
+                for k in range(HALF):
+                    at = pl.ds(pl.multiple_of(k * tall + step * SUB, SUB), SUB)
+                    re, im = spec[at, 0:BLK], spec[at, BLK : 2 * BLK]
+                    cosine, sine = wide(twd[0, k : k + 1, :]), wide(twd[1, k : k + 1, :])
+                    real = re * cosine + im * sine
+                    waves.append((real, None if k in (0, HALF - 1) else re * sine - im * cosine))
+                for k in range(HALF, NBLK):
+                    re, im = waves[NBLK - k]
+                    waves.append((re, -im))
+                removed = fourier(waves, 1)
+                for b in range(NBLK):
+                    done[j, b] = lim[j, b] - removed[b][0]
+
+            for copy in back_copies[part * n_lon : (part + 1) * n_lon]:
+                copy.start()
+
+        inner_tiles()
 
     for g, copies in enumerate(lon_halos):
         for _, receives, copy in copies:
             gated(receives, copy.wait_recv)
-        if g + ahead < groups:
-            send_group(g + ahead)
         sweep(edges, True, [g])
 
     @pl.when(polar)
@@ -495,9 +516,6 @@
             for b in range(nb):
                 at = slice(b * BLK, (b + 1) * BLK)
                 out[pl.ds(ch, SUB), slab_at, at] = jnp.swapaxes(back[:, b, pl.ds(ch, SUB), :], 0, 1)
-
-        for copy in ring_copies:
-            copy.wait_send()
 
     @pl.when(worker)
     def _():
@@ -542,11 +560,11 @@
             pltpu.VMEM((work_rows, NBLK, SUB, BLK), jnp.int32),
             pltpu.VMEM((work_rows, HALF, SUB, BLK), jnp.float32),
             pltpu.VMEM((work_rows, NBLK, SUB, BLK), jnp.float32),
-            pltpu.VMEM((HALF * work_rows * SUB, 2 * BLK), jnp.float32),
+            pltpu.VMEM((HALF * work_rows // PARTS * SUB, 2 * BLK), jnp.float32),
             pltpu.VMEM((work_rows, NBLK, SUB, BLK), jnp.float32),
             pltpu.VMEM((PROWS, cells // BLK, channels, BLK), jnp.float32),
             dma((42,)), dma((42,)),
-        ] + [dma((n_lon,))] * 8 + [dma((10,))],
+        ] + [dma((n_lon,))] * 6 + [dma((PARTS * n_lon,))] * 2 + [dma((10,))],
         compiler_params=pltpu.CompilerParams(
             collective_id=0, has_side_effects=True, vmem_limit_bytes=VMEM_LIMIT
         ),

time: 39 us -> 43 us (1.10); the launches traced: 38.4 us -> 42.9 us
  Pallas kernels: 37 us -> 41.5 us
    pallas_call x1, Pallas kernels: 37 us -> 41.5 us  [body(): pl.pallas_call(functools.partial(kernel, n_lat, n_lon), out_shape=jax.Sha...]
where the time goes in v3:
time: 43 us; the launch traced here: 42.9 us
  Pallas kernels  41.5 us (97%)
  local copies, waits for them, and re-layouts  1.32 us (3%)
    pallas_call x1, Pallas kernels, body(): pl.pallas_call(functools.partial(kernel, n_lat, n_lon), out_shape=jax.Sha...  41.5 us
    unnamed x1, local copies, waits for them, and re-layouts  1.32 us

profile of v3, /device:TPU:0, one launch (start us, length us, event | category | flops | bytes accessed | tf_op | source)
XLA Modules:
  0.0 42.9 jit_solution(10168582609465650828)
XLA Ops:
  0.0 41.5 %shard_map.73 = f32[32,32,512]{2,1,0:T(8,128)S(1)} custom-call(s32[4,32]{1,0:T(4,128)} %bitcast.1, s32[2,8]{1,0:T(2,128)} %cut_h.1, f32[32,32,512]{2,1,0:T(8,128)} %trc_h.1, s32[32,512]{1,0:T(8,128)} %off_h.1, f32[32,512]{1,0:T(8,128)} %frac_h.1, f32[256,256]{1,0:T(8,128)} %constant.4.clone.mat_h, f32[2,16,128]{2,1,0:T(8,128)} %constant.5.clone.twd_h), custom_call_target="tpu_custom_call" | custom-call | flops 1000000000 | bytes 5000000 | tf_op jit(solution)/shard_map/pallas_call | solution.py:539
  41.6 1.3 %copy.9 = f32[32,32,512]{2,1,0:T(8,128)} copy(f32[32,32,512]{2,1,0:T(8,128)S(1)} %shard_map.73) | data formatting | bytes 4194304

commit v4 on v3

--- a/solution.py
+++ b/solution.py
@@ -17,6 +17,7 @@
 SUB = 8
 HALF = NBLK // 2 + 1
 PARTS = 2
+EARLY = 1
 MESH = pl.DeviceIdType.MESH
 VMEM_LIMIT = 48 * 2**20
 
@@ -311,15 +312,15 @@
             copy.start()
         turn(edges + middle, every, True)
 
-    def send_lon(only_polar):
-        for copies in lon_halos:
-            for sends, _, copy in copies:
-                if all(copy is not other for _, _, other in passed) and (sends is polar) == only_polar:
+    def send_lon(chosen):
+        for g in chosen:
+            for sends, _, copy in lon_halos[g]:
+                if all(copy is not other for _, _, other in passed):
                     gated(sends, copy.start)
 
     for sends, _, copy in rims:
         gated(sends, copy.start)
-    send_lon(False)
+    send_lon(range(EARLY))
 
     @pl.when(jnp.logical_not(polar))
     def _():
@@ -389,13 +390,6 @@
     def _():
         inner_tiles()
 
-    @pl.when(polar)
-    def _():
-        for copy in ring_copies:
-            copy.wait_send()
-
-    send_lon(True)
-
     @pl.when(worker)
     def _():
         for copy in tables:
@@ -426,9 +420,11 @@
                 damping = 1.0 - kappa / jnp.maximum(wave, 1).astype(jnp.float32)
                 damp[j, k] = jnp.where(kept, jnp.maximum(damping, 0.0), 0.0) * (1.0 / NLON)
 
+        inner_tiles()
         fetch.wait()
         for n in range(2, len(ring_copies), 3):
             ring_copies[n].wait_recv()
+        send_lon(range(EARLY, groups))
 
         def transform():
             upper, lower = halves(spec[...])
@@ -498,11 +494,15 @@
             for copy in back_copies[part * n_lon : (part + 1) * n_lon]:
                 copy.start()
 
-        inner_tiles()
-
     for g, copies in enumerate(lon_halos):
         for _, receives, copy in copies:
             gated(receives, copy.wait_recv)
+        if g == 0:
+
+            @pl.when(jnp.logical_not(worker))
+            def _():
+                send_lon(range(EARLY, groups))
+
         sweep(edges, True, [g])
 
     @pl.when(polar)
@@ -516,6 +516,9 @@
             for b in range(nb):
                 at = slice(b * BLK, (b + 1) * BLK)
                 out[pl.ds(ch, SUB), slab_at, at] = jnp.swapaxes(back[:, b, pl.ds(ch, SUB), :], 0, 1)
+
+        for copy in ring_copies:
+            copy.wait_send()
 
     @pl.when(worker)
     def _():

time: 43 us -> 39.9 us (0.928)
  Pallas kernels: 41.5 us -> 38.4 us
    pallas_call x1, Pallas kernels: 41.5 us -> 38.4 us  [body(): pl.pallas_call(functools.partial(kernel, n_lat, n_lon), out_shape=jax.Sha...]
where the time goes in v4:
time: 39.9 us; the launch traced here: 39.7 us
  Pallas kernels  38.4 us (96%)
  local copies, waits for them, and re-layouts  1.32 us (3%)
    pallas_call x1, Pallas kernels, body(): pl.pallas_call(functools.partial(kernel, n_lat, n_lon), out_shape=jax.Sha...  38.4 us
    unnamed x1, local copies, waits for them, and re-layouts  1.32 us

profile of v4, /device:TPU:0, one launch (start us, length us, event | category | flops | bytes accessed | tf_op | source)
XLA Modules:
  0.0 39.7 jit_solution(11642085648686971193)
XLA Ops:
  0.0 38.4 %shard_map.73 = f32[32,32,512]{2,1,0:T(8,128)S(1)} custom-call(s32[4,32]{1,0:T(4,128)} %bitcast.1, s32[2,8]{1,0:T(2,128)} %cut_h.1, f32[32,32,512]{2,1,0:T(8,128)} %trc_h.1, s32[32,512]{1,0:T(8,128)} %off_h.1, f32[32,512]{1,0:T(8,128)} %frac_h.1, f32[256,256]{1,0:T(8,128)} %constant.4.clone.mat_h, f32[2,16,128]{2,1,0:T(8,128)} %constant.5.clone.twd_h), custom_call_target="tpu_custom_call" | custom-call | flops 1000000000 | bytes 5000000 | tf_op jit(solution)/shard_map/pallas_call | solution.py:542
  38.4 1.3 %copy.9 = f32[32,32,512]{2,1,0:T(8,128)} copy(f32[32,32,512]{2,1,0:T(8,128)S(1)} %shard_map.73) | data formatting | bytes 4194304

commit v5 on v4

--- a/solution.py
+++ b/solution.py
@@ -17,7 +17,7 @@
 SUB = 8
 HALF = NBLK // 2 + 1
 PARTS = 2
-EARLY = 1
+PIECES = 4
 MESH = pl.DeviceIdType.MESH
 VMEM_LIMIT = 48 * 2**20
 
@@ -232,12 +232,21 @@
         ring_copies += [
             remote(ids_out, ids.at[lon], idx_send.at[d], idx_recv.at[d], (mate, peer)),
             remote(frac.at[slab_at], fracs.at[lon], frc_send.at[d], frc_recv.at[d], (mate, peer)),
-            remote(
-                mid.at[pl.ds(HL + slab, PROWS), :, pl.ds(group_of(peer), SUB), :],
-                ring.at[:, own],
-                pol_send.at[d], pol_recv.at[d], (mate, peer),
-            ),
         ]
+
+    piece_rows = PROWS // PIECES
+    for piece in range(PIECES):
+        for d, peer in enumerate(peers):
+            ring_copies.append(
+                remote(
+                    mid.at[
+                        pl.ds(HL + slab + piece * piece_rows, piece_rows), :,
+                        pl.ds(group_of(peer), SUB), :,
+                    ],
+                    ring.at[pl.ds(piece * piece_rows, piece_rows), own],
+                    pol_send.at[piece * n_lon + d], pol_recv.at[piece * n_lon + d], (mate, peer),
+                )
+            )
 
     for part in range(PARTS):
         for d, peer in enumerate(peers):
@@ -320,7 +329,7 @@
 
     for sends, _, copy in rims:
         gated(sends, copy.start)
-    send_lon(range(EARLY))
+    send_lon(range(groups))
 
     @pl.when(jnp.logical_not(polar))
     def _():
@@ -394,9 +403,8 @@
     def _():
         for copy in tables:
             copy.wait()
-        for n in range(0, len(ring_copies), 3):
-            ring_copies[n].wait_recv()
-            ring_copies[n + 1].wait_recv()
+        for copy in ring_copies[: 2 * n_lon]:
+            copy.wait_recv()
         fetch = pltpu.make_async_copy(
             ids.at[:, pl.ds(PROWS, PROWS), pl.ds(0, BLK)], ids_s, loc_sem.at[9]
         )
@@ -422,9 +430,8 @@
 
         inner_tiles()
         fetch.wait()
-        for n in range(2, len(ring_copies), 3):
-            ring_copies[n].wait_recv()
-        send_lon(range(EARLY, groups))
+        for copy in ring_copies[2 * n_lon :]:
+            copy.wait_recv()
 
         def transform():
             upper, lower = halves(spec[...])
@@ -497,12 +504,6 @@
     for g, copies in enumerate(lon_halos):
         for _, receives, copy in copies:
             gated(receives, copy.wait_recv)
-        if g == 0:
-
-            @pl.when(jnp.logical_not(worker))
-            def _():
-                send_lon(range(EARLY, groups))
-
         sweep(edges, True, [g])
 
     @pl.when(polar)
@@ -567,7 +568,7 @@
             pltpu.VMEM((work_rows, NBLK, SUB, BLK), jnp.float32),
             pltpu.VMEM((PROWS, cells // BLK, channels, BLK), jnp.float32),
             dma((42,)), dma((42,)),
-        ] + [dma((n_lon,))] * 6 + [dma((PARTS * n_lon,))] * 2 + [dma((10,))],
+        ] + [dma((PIECES * n_lon,))] * 2 + [dma((n_lon,))] * 4 + [dma((PARTS * n_lon,))] * 2 + [dma((10,))],
         compiler_params=pltpu.CompilerParams(
             collective_id=0, has_side_effects=True, vmem_limit_bytes=VMEM_LIMIT
         ),

time: 39.9 us -> 39.6 us (level); the launches traced: 39.7 us -> 38.8 us
  Pallas kernels: 38.4 us -> 37.5 us
    pallas_call x1, Pallas kernels: 38.4 us -> 37.5 us  [body(): pl.pallas_call(functools.partial(kernel, n_lat, n_lon), out_shape=jax.Sha...]
where the time goes in v5:
time: 39.6 us; the launch traced here: 38.8 us
  Pallas kernels  37.5 us (95%)
  local copies, waits for them, and re-layouts  1.32 us (3%)
    pallas_call x1, Pallas kernels, body(): pl.pallas_call(functools.partial(kernel, n_lat, n_lon), out_shape=jax.Sha...  37.5 us
    unnamed x1, local copies, waits for them, and re-layouts  1.32 us

profile of v5, /device:TPU:0, one launch (start us, length us, event | category | flops | bytes accessed | tf_op | source)
XLA Modules:
  0.0 38.8 jit_solution(9363337328521903736)
XLA Ops:
  0.0 37.5 %shard_map.73 = f32[32,32,512]{2,1,0:T(8,128)S(1)} custom-call(s32[4,32]{1,0:T(4,128)} %bitcast.1, s32[2,8]{1,0:T(2,128)} %cut_h.1, f32[32,32,512]{2,1,0:T(8,128)} %trc_h.1, s32[32,512]{1,0:T(8,128)} %off_h.1, f32[32,512]{1,0:T(8,128)} %frac_h.1, f32[256,256]{1,0:T(8,128)} %constant.4.clone.mat_h, f32[2,16,128]{2,1,0:T(8,128)} %constant.5.clone.twd_h), custom_call_target="tpu_custom_call" | custom-call | flops 1000000000 | bytes 5000000 | tf_op jit(solution)/shard_map/pallas_call | solution.py:543
  37.5 1.3 %copy.9 = f32[32,32,512]{2,1,0:T(8,128)} copy(f32[32,32,512]{2,1,0:T(8,128)S(1)} %shard_map.73) | data formatting | bytes 4194304
